TPU v7x, 32 devices: a whole 2x2x4 slice. The times are simulated.
32 devices in a mesh: groups: 2 (over y), seq: 8 (over z, x), head: 2 (over core).
Axes of the slice: x: 2, y: 2, z: 4, core: 2. Of those that a mesh axis runs over, the one named last changes fastest.
Arguments:
- text_query_rows: bfloat16 [2048, 8192], P(('groups', 'seq'), 'head'), parts along dimension 0, may hold values from -40 to 40, as said below
- text_key_value: bfloat16 [2, 2048, 1024], P(None, ('groups', 'seq'), 'head'), parts along dimension 1, may hold values from -4 to 4, as said below
- doc_ids: int32 [2048], P(('groups', 'seq')), parts along dimension 0, may hold values from 0 to 3, never falling along the last dimension, each value on 1 to 512 neighbouring positions
- tile_span: int32 [2048, 2], P(('groups', 'seq')), parts along dimension 0, may hold values from 0 to 8, as said below
- vision_hidden: bfloat16 [4096, 1280], P(('groups', 'seq')), parts along dimension 0, may hold values from -6 to 6
- vision_qkv: bfloat16 [3, 4096, 1280], P(None, ('groups', 'seq'), 'head'), parts along dimension 1, may hold values from -6 to 6, as said below
- vision_out_weight: bfloat16 [1280, 1280], P('head'), may hold values from -0.625 to 0.625
- cross_keyvalue_weight: bfloat16 [1280, 2, 1024], P('seq', None, 'head'), may hold values from -0.15625 to 0.15625
- cross_gate: float32 [64], P('head'), may hold values from -1.5 to 1.5
Outputs:
- attention_out: bfloat16 [2048, 8192], P(('groups', 'seq'), 'head'), parts along dimension 0
There are 2 independent parts, one for each index of `groups`. A program takes and returns all parts, laid end to end along the dimension named above; an argument that names none is the same for every part. Nothing has to cross between parts.
Inputs may be any that keep to these rules, and one draw needn't show every extreme that they name: `tile_span`: each text token's span is an interval of the tiles of its own block b = p // 128 and of block b - 1 (first <= second, both between b - 1 and b + 1, never below 0); it may be empty. `doc_ids`: never falling along the document; each segment holds 1 to 512 tokens. `text_query_rows`: real values. `text_key_value`: real values. `vision_qkv`: real values.
All inputs are finite; a program needn't handle non-finite values.
Results may differ from a plain program's by a relative error of at most 0.024.
Values may be sent and summed in bfloat16 or wider, within the bound.
A program may use at most 64 MiB of HBM per device.

v0:
```python
import math
import jax
import jax.numpy as jnp
from jax import lax
from jax.sharding import PartitionSpec as P

HEAD_SIZE = 128
VHD = 80
WINDOW_BLOCKS = 2


def passed_along(block, axis, distance):
    devices = range(lax.axis_size(axis))
    route = [(i - distance, i) for i in devices if i - distance in devices]
    return lax.ppermute(block, axis, route)


def attend_heads(query_rows, keys, allowed_mask):
    scores = jnp.einsum(
        "tgrd,kgd->grtk", query_rows, keys, preferred_element_type=jnp.float32
    ) / math.sqrt(HEAD_SIZE)
    scores = jnp.where(allowed_mask[None, None], scores, -1e30)
    return jax.nn.softmax(scores, axis=-1)


def per_device(
    text_query_rows,
    text_key_value,
    doc_ids,
    tile_span,
    vision_hidden,
    vision_qkv,
    vision_out_weight,
    cross_keyvalue_weight,
    cross_gate,
):
    text_rows = text_query_rows.shape[0]
    tile_rows = vision_hidden.shape[0]
    kv_cols = text_key_value.shape[2]
    kv_heads = kv_cols // HEAD_SIZE
    query_group_ratio = text_query_rows.shape[1] // HEAD_SIZE // kv_heads
    seq_index = lax.axis_index("seq")
    vision_query = vision_qkv[0].reshape(tile_rows, -1, VHD)
    vision_key = vision_qkv[1].reshape(tile_rows, -1, VHD)
    vision_value = vision_qkv[2].reshape(tile_rows, -1, VHD)
    vision_scores = jnp.einsum(
        "qhd,khd->hqk", vision_query, vision_key, preferred_element_type=jnp.float32
    ) / math.sqrt(VHD)
    vision_weights = jax.nn.softmax(vision_scores, axis=-1).astype(jnp.bfloat16)
    vision_attn = jnp.einsum(
        "hqk,khd->qhd", vision_weights, vision_value, preferred_element_type=jnp.float32
    )
    vision_attn = vision_attn.astype(jnp.bfloat16).reshape(tile_rows, -1)
    partial_mix = jnp.dot(vision_attn, vision_out_weight, preferred_element_type=jnp.float32)
    mixed_sum = lax.psum(partial_mix, "head") + vision_hidden.astype(jnp.float32)
    image_norm = (
        mixed_sum * lax.rsqrt(jnp.mean(mixed_sum * mixed_sum, axis=-1, keepdims=True) + 1e-05)
    ).astype(jnp.bfloat16)
    image_key_value = jnp.einsum(
        "ic,cjf->ijf",
        image_norm,
        lax.all_gather(cross_keyvalue_weight, "seq", axis=0, tiled=True),
        preferred_element_type=jnp.float32,
    ).astype(jnp.bfloat16)
    earlier_tile = passed_along(image_key_value, "seq", 1)
    blocks = [(text_key_value, doc_ids)]
    current_kv, current_docs = (text_key_value, doc_ids)
    for repeat_count in range(WINDOW_BLOCKS):
        current_kv, current_docs = passed_along((current_kv, current_docs), "seq", 1)
        blocks.insert(0, (current_kv, current_docs))
    all_keyval = jnp.concatenate([member[0] for member in blocks], axis=1)
    all_docs = jnp.concatenate([member[1] for member in blocks], axis=0)
    key_pos = (seq_index - WINDOW_BLOCKS) * text_rows + jnp.arange(
        (WINDOW_BLOCKS + 1) * text_rows, dtype=jnp.int32
    )
    query_pos = seq_index * text_rows + jnp.arange(text_rows, dtype=jnp.int32)
    allowed_mask = (
        (all_docs[None, :] == doc_ids[:, None])
        & (key_pos[None, :] <= query_pos[:, None])
        & (key_pos[None, :] >= 0)
    )
    query_rows = text_query_rows.reshape(text_rows, kv_heads, query_group_ratio, HEAD_SIZE)
    self_attention_weights = attend_heads(
        query_rows, all_keyval[0].reshape(-1, kv_heads, HEAD_SIZE), allowed_mask
    ).astype(jnp.bfloat16)
    self_output = jnp.einsum(
        "ycmq,qyb->mycb",
        self_attention_weights,
        all_keyval[1].reshape(-1, kv_heads, HEAD_SIZE),
        preferred_element_type=jnp.float32,
    )
    self_output = self_output.reshape(text_rows, -1)
    image_all = jnp.concatenate([earlier_tile, image_key_value], axis=0)
    tile_ids = seq_index - 1 + jnp.arange(2 * tile_rows, dtype=jnp.int32) // tile_rows
    low_tile = tile_span[:, 0]
    high_tile = tile_span[:, 1]
    visible_mask = (tile_ids[None, :] >= low_tile[:, None]) & (
        tile_ids[None, :] < high_tile[:, None]
    )
    image_present = (high_tile > low_tile).astype(jnp.float32)
    cross_probabilities = (
        attend_heads(query_rows, image_all[:, 0].reshape(-1, kv_heads, HEAD_SIZE), visible_mask)
        * image_present[None, None, :, None]
    )
    cross_probabilities = cross_probabilities.astype(jnp.bfloat16)
    cross_output = jnp.einsum(
        "ycmq,qyb->mycb",
        cross_probabilities,
        image_all[:, 1].reshape(-1, kv_heads, HEAD_SIZE),
        preferred_element_type=jnp.float32,
    )
    cross_output = cross_output.reshape(text_rows, -1)
    gate_cols = jnp.repeat(jnp.tanh(cross_gate), HEAD_SIZE)
    return (self_output + gate_cols[None, :] * cross_output).astype(jnp.bfloat16)


def solution(mesh):
    placed = (
        P(("groups", "seq"), "head"),
        P(None, ("groups", "seq"), "head"),
        P(("groups", "seq")),
        P(("groups", "seq"), None),
        P(("groups", "seq"), None),
        P(None, ("groups", "seq"), "head"),
        P("head", None),
        P("seq", None, "head"),
        P("head"),
    )
    return jax.shard_map(
        per_device,
        mesh=mesh,
        in_specs=placed,
        out_specs=P(("groups", "seq"), "head"),
        check_vma=False,
    )
```

profile of v0, /device:TPU:8, one launch (start us, length us, event | category | flops | bytes accessed | tf_op | source)
XLA Modules:
  0.0 130.6 jit_solution(16018390959418832903)
XLA Ops:
  7.4 1.4 %fusion.35 = (bf16[1,256,640]{2,1,0:T(8,128)(2,1)S(1)}, bf16[1,256,640]{2,1,0:T(8,128)(2,1)S(1)}, bf16[1,256,640]{2,1,0:T(8,128)(2,1)S(1)}) fusion(bf16[3,256,640]{2,1,0:T(8,128)(2,1)} %param.14), kind=kLoop, calls=%fused_computation.67 | loop fusion | bytes 1966080 | tf_op jit(solution)/shard_map/slice | solution.py:44
  8.8 0.2 copy.30
  9.3 2.2 %fusion.38 = (f32[8,256]{1,0:T(8,128)S(1)}, f32[8,256,256]{1,2,0:T(8,128)}) fusion(bf16[256,8,80]{0,2,1:T(8,128)(2,1)S(1)} %bitcast.88, bf16[256,8,80]{0,2,1:T(8,128)(2,1)S(1)} %bitcast.87), kind=kOutput, calls=%fused_computation.70 | convolution fusion | flops 85459200 | bytes 2760704 | tf_op jit(solution)/shard_map/sub | solution.py:49
  11.5 1.9 %convolution_convert_fusion.1 = bf16[8,256,80]{1,2,0:T(8,128)(2,1)S(1)} fusion(bf16[256,8,80]{0,2,1:T(8,128)(2,1)S(1)} %bitcast.89, f32[8,256,256]{1,2,0:T(8,128)} %get-tuple-element.17, f32[8,256]{1,0:T(8,128)S(1)} %get-tuple-element.16), kind=kOutput, calls=%fused_computation.28 | convolution fusion | flops 85098496 | bytes 2760704 | tf_op jit(solution)/shard_map/hqk,khd->qhd/dot_general | solution.py:50
  13.4 1.8 %fusion.40 = f32[256,1280]{1,0:T(8,128)} fusion(bf16[256,640]{0,1:T(8,128)(2,1)S(1)} %bitcast.86, bf16[640,1280]{1,0:T(8,128)(2,1)S(1)} %copy-done), kind=kOutput, calls=%fused_computation.72 | convolution fusion | flops 419430400 | bytes 3276800 | tf_op jit(solution)/shard_map/dot_general | solution.py:54
  15.3 0.8 copy.33
  16.1 3.4 %collective-permute-start.2 = (s32[128]{0:T(128)S(1)}, s32[128]{0:T(128)S(1)}, u32[]{:S(2)}, u32[]{:S(2)}) collective-permute-start(s32[128]{0:T(128)S(1)} %copy-done.5), channel_id=1, source_target_pairs={{0,2},{2,4},{4,6},{6,8},{8,10},{10,12},{12,14},{1,3},{3,5},{5,7},{... | collective-permute-start | bytes 1544 | tf_op jit(solution)/shard_map/ppermute | solution.py:15
  19.7 3.5 %collective-permute-start = (bf16[2,128,512]{1,2,0:T(8,128)(2,1)S(1)}, bf16[2,128,512]{1,2,0:T(8,128)(2,1)S(1)}, u32[]{:S(2)}, u32[]{:S(2)}) collective-permute-start(bf16[2,128,512]{1,2,0:T(8,128)(2,1)S(1)} %copy.24), channel_id=1, source_target_pairs={{0,2},{2,4},{4,6},{6,8},{8,10},{10,12},{12,14},{1,3},{3,5},{5,7},{... | collective-permute-start | bytes 786440 | tf_op jit(solution)/shard_map/ppermute | solution.py:15
  23.5 3.4 %collective-permute-start.3 = (s32[128]{0:T(128)S(1)}, s32[128]{0:T(128)S(1)}, u32[]{:S(2)}, u32[]{:S(2)}) collective-permute-start(s32[128]{0:T(128)S(1)} %collective-permute-done.2), channel_id=1, source_target_pairs={{0,2},{2,4},{4,6},{6,8},{8,10},{10,12},{12,14},{1,3},{3,5},{5,7},{... | collective-permute-start | bytes 1544 | tf_op jit(solution)/shard_map/ppermute | solution.py:15
  26.9 1.5 %copy.52 = bf16[16,8,32,128]{3,2,1,0:T(8,128)(2,1)S(1)} copy(bf16[16,8,32,128]{3,1,2,0:T(8,128)(2,1)} %bitcast.83) | data formatting | bytes 2097152
  28.4 2.6 %collective-permute-done = bf16[2,128,512]{1,2,0:T(8,128)(2,1)S(1)} collective-permute-done((bf16[2,128,512]{1,2,0:T(8,128)(2,1)S(1)}, bf16[2,128,512]{1,2,0:T(8,128)(2,1)S(1)}, u32[]{:S(2)}, u32[]{:S(2)}) %collective-permute-start) | collective-permute-done | bytes 262176 | tf_op jit(solution)/shard_map/ppermute | solution.py:15
  30.9 3.1 %collective-permute-start.1 = (bf16[2,128,512]{1,2,0:T(8,128)(2,1)S(1)}, bf16[2,128,512]{1,2,0:T(8,128)(2,1)S(1)}, u32[]{:S(2)}, u32[]{:S(2)}) collective-permute-start(bf16[2,128,512]{1,2,0:T(8,128)(2,1)S(1)} %collective-permute-done), channel_id=1, source_target_pairs={{0,2},{2,4},{4,6},{6,8},{8,10},{10,12},{12,14},{1,3},{3,5},{5,7},{... | collective-permute-start | bytes 786440 | tf_op jit(solution)/shard_map/ppermute | solution.py:15
  34.0 0.2 and_and_fusion
  34.2 12.1 %collective-permute-done.1 = bf16[2,128,512]{1,2,0:T(8,128)(2,1)S(1)} collective-permute-done((bf16[2,128,512]{1,2,0:T(8,128)(2,1)S(1)}, bf16[2,128,512]{1,2,0:T(8,128)(2,1)S(1)}, u32[]{:S(2)}, u32[]{:S(2)}) %collective-permute-start.1) | collective-permute-done | bytes 262176 | tf_op jit(solution)/shard_map/ppermute | solution.py:15
  46.5 0.8 fusion.36
  47.3 1.0 fusion.17
  48.4 3.7 %fusion.37 = (f32[4,8,128]{2,1,0:T(8,128)S(1)}, f32[4,8,128,384]{2,3,1,0:T(8,128)}) fusion(f32[4,384,128,8]{2,1,3,0:T(8,128)S(1)} %fusion.17, pred[128,384]{0,1:T(8,128)(4,1)S(1)} %and_and_fusion), kind=kOutput, calls=%fused_computation.69 | output fusion | flops 9437567 | bytes 12648448 | tf_op jit(solution)/shard_map/sub | solution.py:23
  52.1 1.6 %multiply_reduce_fusion.1 = f32[256]{0:T(256)S(1)} fusion(f32[256,1280]{1,0:T(8,128)} %all-reduce.2.cloned.1.call-done, bf16[256,1280]{1,0:T(8,128)(2,1)S(1)} %copy-done.1), kind=kLoop, calls=%fused_computation.25 | loop fusion | flops 1310464 | bytes 1967104 | tf_op jit(solution)/shard_map/reduce_sum | solution.py:57
  53.7 23.4 %all-gather.2.cloned.1.call-done = bf16[1280,2,512]{2,0,1:T(8,128)(2,1)} async-done(((bf16[160,2,512]{2,0,1:T(8,128)(2,1)}), bf16[1280,2,512]{2,0,1:T(8,128)(2,1)}) %all-gather.2.cloned.1.call-update) | async-done | bytes 2621456 | tf_op jit(solution)/shard_map/all_gather | solution.py:62
  77.1 3.9 %convolution_convert_fusion = bf16[256,2,512]{2,0,1:T(8,128)(2,1)} fusion(bf16[1280,2,512]{2,0,1:T(8,128)(2,1)} %all-gather.2.cloned.1.call-done, f32[256,1280]{1,0:T(8,128)} %all-reduce.2.cloned.1.call-done, bf16[256,1280]{1,0:T(8,128)(2,1)S(1)} %copy-done.1, f32[256]{0:T(256)S(1)} %add_rsqrt_fusion), kind=kOutput, calls=%fused_computation.27 | convolution fusion | flops 672661504 | bytes 5112832 | tf_op jit(solution)/shard_map/ic,cjf->ijf/dot_general | solution.py:59
  81.0 2.6 %collective-permute-start.4 = (bf16[256,2,512]{2,0,1:T(8,128)(2,1)}, bf16[256,2,512]{2,0,1:T(8,128)(2,1)S(1)}, u32[]{:S(2)}, u32[]{:S(2)}) collective-permute-start(bf16[256,2,512]{2,0,1:T(8,128)(2,1)} %convolution_convert_fusion), channel_id=1, source_target_pairs={{0,2},{2,4},{4,6},{6,8},{8,10},{10,12},{12,14},{1,3},{3,5},{5,7},{... | collective-permute-start | bytes 1572872 | tf_op jit(solution)/shard_map/ppermute | solution.py:15
  83.6 4.9 %fusion.11 = f32[4,128,8,128]{3,1,2,0:T(8,128)} fusion(bf16[384,4,128,1]{0,2,3,1:T(8,128)(2,1)S(1)} %bitcast.85, f32[4,8,128,384]{2,3,1,0:T(8,128)} %get-tuple-element.15, f32[4,8,128]{2,1,0:T(8,128)S(1)} %get-tuple-element.14), kind=kOutput, calls=%fused_computation.17 | convolution fusion | flops 405798912 | bytes 8798208 | tf_op jit(solution)/shard_map/ycmq,qyb->mycb/dot_general | solution.py:86
  88.5 2.9 %copy.39 = f32[128,4096]{1,0:T(8,128)} copy(f32[128,4096]{0,1:T(8,128)} %bitcast.81) | data formatting | bytes 4194304 | tf_op jit(solution)/shard_map/reshape | solution.py:92
  91.5 5.0 %collective-permute-done.4 = bf16[256,2,512]{2,0,1:T(8,128)(2,1)S(1)} collective-permute-done((bf16[256,2,512]{2,0,1:T(8,128)(2,1)}, bf16[256,2,512]{2,0,1:T(8,128)(2,1)S(1)}, u32[]{:S(2)}, u32[]{:S(2)}) %collective-permute-start.4) | collective-permute-done | bytes 524320 | tf_op jit(solution)/shard_map/ppermute | solution.py:15
  96.5 2.1 %pad_maximum_fusion.1 = (bf16[512,1,512]{2,0,1:T(8,128)(2,1)}, bf16[512,1,512]{2,0,1:T(8,128)(2,1)}) fusion(bf16[256,2,512]{2,0,1:T(8,128)(2,1)} %convolution_convert_fusion, bf16[256,2,512]{2,0,1:T(8,128)(2,1)S(1)} %collective-permute-done.4), kind=kLoop, calls=%fused_computation.40 | loop fusion | flops 2097152 | bytes 2097152 | tf_op jit(solution)/shard_map/concatenate | solution.py:93
  98.6 1.2 reshape_squeeze.27
  99.8 4.5 %fusion.15 = f32[4,512,128,8]{2,1,3,0:T(8,128)} fusion(bf16[128,4,8,128]{3,2,1,0:T(8,128)(2,1)S(1)} %bitcast.78, bf16[512,4,128,1]{2,1,0,3:T(4,128)(2,1)S(1)} %bitcast.79), kind=kOutput, calls=%fused_computation.32 | convolution fusion | flops 536870912 | bytes 9961472 | tf_op jit(solution)/shard_map/tgrd,kgd->grtk/dot_general | solution.py:19
  104.3 1.3 copy.49
  105.5 8.9 %fusion.39 = (f32[4,8,128]{2,1,0:T(8,128)S(1)}, f32[4,8,128,512]{2,3,1,0:T(8,128)S(1)}) fusion(f32[4,512,128,8]{2,1,3,0:T(8,128)} %fusion.15, pred[128,512]{0,1:T(8,128)(4,1)S(1)} %compare_and_fusion), kind=kOutput, calls=%fused_computation.71 | output fusion | flops 12583423 | bytes 16859136 | tf_op jit(solution)/shard_map/sub | solution.py:23
  114.4 2.3 %fusion.8 = f32[4,128,8,128]{3,1,2,0:T(8,128)} fusion(bf16[512,4,128,1]{0,2,3,1:T(8,128)(2,1)S(1)} %bitcast.84, f32[4,8,128,512]{2,3,1,0:T(8,128)S(1)} %get-tuple-element.19, f32[128]{0:T(128)S(1)} %compare_convert_fusion, f32[4,8,128]{2,1,0:T(8,128)S(1)} %get-tuple-element.18), kind=kOutput, calls=%fused_computation.14 | convolution fusion | flops 543162368 | bytes 11026944 | tf_op jit(solution)/shard_map/ycmq,qyb->mycb/dot_general | solution.py:106
  116.8 2.9 %copy.38 = f32[128,4096]{1,0:T(8,128)} copy(f32[128,4096]{0,1:T(8,128)} %bitcast.80) | data formatting | bytes 4194304 | tf_op jit(solution)/shard_map/reshape | solution.py:112
  119.7 3.5 %add_convert_fusion = bf16[128,4096]{1,0:T(8,128)(2,1)} fusion(f32[128,4096]{1,0:T(8,128)} %copy.39, f32[128,4096]{1,0:T(8,128)} %copy.38, f32[4096]{0:T(1024)S(1)} %broadcast_bitcast_fusion), kind=kLoop, calls=%fused_computation.19 | loop fusion | flops 1572864 | bytes 5259264 | tf_op jit(solution)/shard_map/convert_element_type | solution.py:114
  (38 shorter events, 1.0 us)
Async XLA Ops:
  7.4 6.0 %copy-start = (bf16[640,1280]{1,0:T(8,128)(2,1)S(1)}, bf16[640,1280]{1,0:T(8,128)(2,1)}, u32[]{:S(2)}) copy-start(bf16[640,1280]{1,0:T(8,128)(2,1)} %param.15) | copy-start | bytes 4915204
  7.4 44.7 %all-reduce.2.cloned.1.call-start = ((), (), s32[]{:S(2)}) async-start(), calls=%async_computation | async-start | bytes 2621440 | tf_op jit(solution)/shard_map/psum | solution.py:55
  13.4 1.9 %copy-start.3 = (bf16[160,2,512]{2,1,0:T(2,128)(2,1)S(1)}, bf16[160,2,512]{2,1,0:T(2,128)(2,1)}, u32[]{:S(2)}) copy-start(bf16[160,2,512]{2,1,0:T(2,128)(2,1)} %param.16) | copy-start | bytes 983044
  13.4 2.7 %copy-start.5 = (s32[128]{0:T(128)S(1)}, s32[128]{0:T(128)}, u32[]{:S(2)}) copy-start(s32[128]{0:T(128)} %param.11) | copy-start | bytes 1540
  13.4 6.1 %copy-start.4 = (bf16[2,128,512]{2,1,0:T(8,128)(2,1)S(1)}, bf16[2,128,512]{2,1,0:T(8,128)(2,1)}, u32[]{:S(2)}) copy-start(bf16[2,128,512]{2,1,0:T(8,128)(2,1)} %param.10) | copy-start | bytes 786436
  13.4 9.7 %copy-start.7 = (f32[32]{0:T(128)S(1)}, f32[32]{0:T(128)}, u32[]{:S(2)}) copy-start(f32[32]{0:T(128)} %param.17) | copy-start | bytes 388
  13.4 9.8 %copy-start.6 = (s32[128,2]{0,1:T(2,128)S(1)}, s32[128,2]{0,1:T(2,128)}, u32[]{:S(2)}) copy-start(s32[128,2]{0,1:T(2,128)} %param.12) | copy-start | bytes 3076
  15.2 61.9 %all-gather.2.cloned.1.call-start = ((), (), s32[]{:S(2)}) async-start(), calls=%async_computation.1 | async-start | bytes 2949120 | tf_op jit(solution)/shard_map/all_gather | solution.py:62
  16.1 7.4 %collective-permute-start.2 = (s32[128]{0:T(128)S(1)}, s32[128]{0:T(128)S(1)}, u32[]{:S(2)}, u32[]{:S(2)}) collective-permute-start(s32[128]{0:T(128)S(1)} %copy-done.5), channel_id=1, source_target_pairs={{0,2},{2,4},{4,6},{6,8},{8,10},{10,12},{12,14},{1,3},{3,5},{5,7},{... | collective-permute-start | bytes 1544 | tf_op jit(solution)/shard_map/ppermute | solution.py:15
  19.7 11.3 %collective-permute-start = (bf16[2,128,512]{1,2,0:T(8,128)(2,1)S(1)}, bf16[2,128,512]{1,2,0:T(8,128)(2,1)S(1)}, u32[]{:S(2)}, u32[]{:S(2)}) collective-permute-start(bf16[2,128,512]{1,2,0:T(8,128)(2,1)S(1)} %copy.24), channel_id=1, source_target_pairs={{0,2},{2,4},{4,6},{6,8},{8,10},{10,12},{12,14},{1,3},{3,5},{5,7},{... | collective-permute-start | bytes 786440 | tf_op jit(solution)/shard_map/ppermute | solution.py:15
  23.5 10.5 %collective-permute-start.3 = (s32[128]{0:T(128)S(1)}, s32[128]{0:T(128)S(1)}, u32[]{:S(2)}, u32[]{:S(2)}) collective-permute-start(s32[128]{0:T(128)S(1)} %collective-permute-done.2), channel_id=1, source_target_pairs={{0,2},{2,4},{4,6},{6,8},{8,10},{10,12},{12,14},{1,3},{3,5},{5,7},{... | collective-permute-start | bytes 1544 | tf_op jit(solution)/shard_map/ppermute | solution.py:15
  30.9 15.5 %collective-permute-start.1 = (bf16[2,128,512]{1,2,0:T(8,128)(2,1)S(1)}, bf16[2,128,512]{1,2,0:T(8,128)(2,1)S(1)}, u32[]{:S(2)}, u32[]{:S(2)}) collective-permute-start(bf16[2,128,512]{1,2,0:T(8,128)(2,1)S(1)} %collective-permute-done), channel_id=1, source_target_pairs={{0,2},{2,4},{4,6},{6,8},{8,10},{10,12},{12,14},{1,3},{3,5},{5,7},{... | collective-permute-start | bytes 786440 | tf_op jit(solution)/shard_map/ppermute | solution.py:15
  48.4 3.7 %copy-start.1 = (bf16[256,1280]{1,0:T(8,128)(2,1)S(1)}, bf16[256,1280]{1,0:T(8,128)(2,1)}, u32[]{:S(2)}) copy-start(bf16[256,1280]{1,0:T(8,128)(2,1)} %param.13) | copy-start | bytes 1966084
  77.1 6.5 %copy-start.2 = (bf16[1,384,512]{1,2,0:T(8,128)(2,1)S(1)}, bf16[1,384,512]{1,2,0:T(8,128)(2,1)}, u32[]{:S(2)}) copy-start(bf16[1,384,512]{1,2,0:T(8,128)(2,1)} %get-tuple-element.11) | copy-start | bytes 1179652
  81.0 15.5 %collective-permute-start.4 = (bf16[256,2,512]{2,0,1:T(8,128)(2,1)}, bf16[256,2,512]{2,0,1:T(8,128)(2,1)S(1)}, u32[]{:S(2)}, u32[]{:S(2)}) collective-permute-start(bf16[256,2,512]{2,0,1:T(8,128)(2,1)} %convolution_convert_fusion), channel_id=1, source_target_pairs={{0,2},{2,4},{4,6},{6,8},{8,10},{10,12},{12,14},{1,3},{3,5},{5,7},{... | collective-permute-start | bytes 1572872 | tf_op jit(solution)/shard_map/ppermute | solution.py:15
Sparse Core Ops, SparseCore 0:
  15.3 21.4 all-reduce.1
Sparse Core Ops, SparseCore 1:
  17.9 59.1 all-gather.1
where the time goes:
time: 131 us
  waiting for transfers between devices  43.2 us (33%)
  matrix products  22.5 us (17%)
  other arithmetic  20.2 us (15%)
  starting transfers between devices  16 us (12%)
  between operations  15.1 us (12%)
  local copies, waits for them, and re-layouts  13.6 us (10%)
    all_gather x1, waiting for transfers between devices, per_device(): lax.all_gather(cross_keyvalue_weight, 'seq', axis=0, tiled=True)  23.4 us
    ppermute x5, waiting for transfers between devices, passed_along(): return lax.ppermute(block, axis, route)  19.7 us
    ppermute x5, starting transfers between devices, passed_along(): return lax.ppermute(block, axis, route)  16 us
    sub x2, other arithmetic, attend_heads(): return jax.nn.softmax(scores, axis=-1)  12.6 us
    dot_general x2, matrix products, attend_heads(): jnp.einsum('tgrd,kgd->grtk', query_rows, keys, preferred_element_type=jnp...  5.54 us
    dot_general x1, matrix products, per_device(): jnp.einsum('ycmq,qyb->mycb', self_attention_weights, all_keyval[1].reshap...  4.89 us
    dot_general x1, matrix products, per_device(): jnp.einsum('ic,cjf->ijf', image_norm, lax.all_gather(cross_keyvalue_weigh...  3.87 us
    convert_element_type x1, other arithmetic, per_device(): (self_output + gate_cols[None, :] * cross_output).astype(jnp.bfloat16)  3.46 us
  transfers between devices with their start and end apart: 7, of which 4 were waited for; matrix products, arithmetic and copies ran while one was open for 14% of the time, Pallas kernels for 0%

commit v1 on v0

--- a/solution.py
+++ b/solution.py
@@ -7,6 +7,22 @@
 HEAD_SIZE = 128
 VHD = 80
 WINDOW_BLOCKS = 2
+
+
+def summed_both_ways(x, axis, dim, term):
+    peers, mine, width = (lax.axis_size(axis), lax.axis_index(axis), x.shape[dim])
+    ahead = [(i, (i + 1) % peers) for i in range(peers)]
+    left = [(i, (i - 1) % peers) for i in range(peers)]
+    half = peers // 2
+    from_left = from_right = x
+    so_far = term(x, mine * width)
+    for hop in range(1, half + 1):
+        from_left = lax.ppermute(from_left, axis, ahead)
+        if hop < peers - half:
+            from_right = lax.ppermute(from_right, axis, left)
+            so_far = so_far + term(from_right, (mine + hop) % peers * width)
+        so_far = so_far + term(from_left, (mine - hop) % peers * width)
+    return so_far
 
 
 def passed_along(block, axis, distance):
@@ -56,11 +72,16 @@
     image_norm = (
         mixed_sum * lax.rsqrt(jnp.mean(mixed_sum * mixed_sum, axis=-1, keepdims=True) + 1e-05)
     ).astype(jnp.bfloat16)
-    image_key_value = jnp.einsum(
-        "ic,cjf->ijf",
-        image_norm,
-        lax.all_gather(cross_keyvalue_weight, "seq", axis=0, tiled=True),
-        preferred_element_type=jnp.float32,
+    image_key_value = summed_both_ways(
+        cross_keyvalue_weight,
+        "seq",
+        0,
+        lambda part, start: jnp.einsum(
+            "ic,cjf->ijf",
+            lax.dynamic_slice_in_dim(image_norm, start, part.shape[0], axis=1),
+            part,
+            preferred_element_type=jnp.float32,
+        ),
     ).astype(jnp.bfloat16)
     earlier_tile = passed_along(image_key_value, "seq", 1)
     blocks = [(text_key_value, doc_ids)]

time: 131 us -> 128 us (0.977)
  waiting for transfers between devices: 43.2 us -> 34.3 us
  starting transfers between devices: 16 us -> 24.7 us
  local copies, waits for them, and re-layouts: 13.6 us -> 9.83 us
  matrix products: 22.5 us -> 23.9 us
    all_gather x1 -> x0, waiting for transfers between devices: 23.4 us -> none  [per_device(): lax.all_gather(cross_keyvalue_weight, 'seq', axis=0, tiled=True)]
    ppermute x0 -> x7, waiting for transfers between devices: none -> 12.9 us  [the longest x3 9.64 us: summed_both_ways(): from_right = lax.ppermute(from_right, axis, left)]
    ppermute x0 -> x7, starting transfers between devices: none -> 9.56 us  [the longest x4 8.13 us: summed_both_ways(): from_left = lax.ppermute(from_left, axis, ahead)]
    dot_general x1 -> x8, matrix products: 3.87 us -> 7.97 us  [per_device(): jnp.einsum('ic,cjf->ijf', lax.dynamic_slice_in_dim(image_norm, start, par...]
    dot_general x1, matrix products: 4.89 us -> 2.09 us  [per_device(): jnp.einsum('ycmq,qyb->mycb', self_attention_weights, all_keyval[1].reshap...]
    concatenate x1, other arithmetic: 2.08 us -> 0.07 us  [per_device(): image_all = jnp.concatenate([earlier_tile, image_key_value], axis=0)]
    ppermute x5, waiting for transfers between devices: 19.7 us -> 21.4 us  [passed_along(): return lax.ppermute(block, axis, route)]
    convert_element_type x0 -> x1, other arithmetic: none -> 1.5 us  [per_device(): image_norm = (mixed_sum * lax.rsqrt(jnp.mean(mixed_sum * mixed_sum, axis=...]
  transfers between devices with their start and end apart: 7 -> 13, of which waited for: 4 -> 6; matrix products, arithmetic and copies ran while one was open for 14% -> 23% of each run, Pallas kernels for 0% -> 0%
where the time goes in v1:
time: 128 us; the launch traced here: 126 us
  waiting for transfers between devices  34.3 us (27%)
  starting transfers between devices  24.7 us (19%)
  matrix products  23.9 us (19%)
  other arithmetic  19.6 us (15%)
  between operations  13.9 us (11%)
  local copies, waits for them, and re-layouts  9.83 us (8%)
    ppermute x5, waiting for transfers between devices, passed_along(): return lax.ppermute(block, axis, route)  21.4 us
    ppermute x5, starting transfers between devices, passed_along(): return lax.ppermute(block, axis, route)  15.2 us
    sub x2, other arithmetic, attend_heads(): return jax.nn.softmax(scores, axis=-1)  12.5 us
    ppermute x3, waiting for transfers between devices, summed_both_ways(): from_right = lax.ppermute(from_right, axis, left)  9.64 us
    ppermute x4, starting transfers between devices, summed_both_ways(): from_left = lax.ppermute(from_left, axis, ahead)  8.13 us
    dot_general x8, matrix products, per_device(): jnp.einsum('ic,cjf->ijf', lax.dynamic_slice_in_dim(image_norm, start, par...  7.97 us
    dot_general x2, matrix products, attend_heads(): jnp.einsum('tgrd,kgd->grtk', query_rows, keys, preferred_element_type=jnp...  5.54 us
    convert_element_type x1, other arithmetic, per_device(): (self_output + gate_cols[None, :] * cross_output).astype(jnp.bfloat16)  3.46 us
  transfers between devices with their start and end apart: 13, of which 6 were waited for; matrix products, arithmetic and copies ran while one was open for 23% of the time, Pallas kernels for 0%

profile of v1, /device:TPU:8, one launch (start us, length us, event | category | flops | bytes accessed | tf_op | source)
XLA Modules:
  0.0 126.3 jit_solution(17028116818884852207)
XLA Ops:
  7.7 1.4 %collective-permute-start.4 = (bf16[160,2,512]{2,0,1:T(8,128)(2,1)S(1)}, bf16[160,2,512]{2,0,1:T(8,128)(2,1)}, u32[]{:S(2)}, u32[]{:S(2)}) collective-permute-start(bf16[160,2,512]{2,0,1:T(8,128)(2,1)S(1)} %copy.44), channel_id=1, source_target_pairs={{0,14},{2,0},{4,2},{6,4},{8,6},{10,8},{12,10},{14,12},{1,15},{3,1}... | collective-permute-start | bytes 983048 | tf_op jit(solution)/shard_map/ppermute | solution.py:22
  11.6 2.2 %fusion.66 = (f32[8,256]{1,0:T(8,128)S(1)}, f32[8,256,256]{1,2,0:T(8,128)}) fusion(bf16[256,8,80]{0,2,1:T(8,128)(2,1)S(1)} %bitcast.115, bf16[256,8,80]{0,2,1:T(8,128)(2,1)S(1)} %bitcast.114), kind=kOutput, calls=%fused_computation.103 | convolution fusion | flops 85459200 | bytes 2760704 | tf_op jit(solution)/shard_map/sub | solution.py:65
  13.7 1.9 %convolution_convert_fusion = bf16[8,256,80]{1,2,0:T(8,128)(2,1)S(1)} fusion(bf16[256,8,80]{0,2,1:T(8,128)(2,1)S(1)} %bitcast.116, f32[8,256,256]{1,2,0:T(8,128)} %get-tuple-element.17, f32[8,256]{1,0:T(8,128)S(1)} %get-tuple-element.16), kind=kOutput, calls=%fused_computation.35 | convolution fusion | flops 85098496 | bytes 2760704 | tf_op jit(solution)/shard_map/hqk,khd->qhd/dot_general | solution.py:66
  15.7 1.9 %fusion.68 = f32[256,1280]{1,0:T(8,128)} fusion(bf16[256,640]{0,1:T(8,128)(2,1)S(1)} %bitcast.113, bf16[640,1280]{1,0:T(8,128)(2,1)S(1)} %copy-done), kind=kOutput, calls=%fused_computation.105 | convolution fusion | flops 419430400 | bytes 3276800 | tf_op jit(solution)/shard_map/dot_general | solution.py:70
  17.6 4.3 %collective-permute-start.2 = (s32[128]{0:T(128)S(1)}, s32[128]{0:T(128)S(1)}, u32[]{:S(2)}, u32[]{:S(2)}) collective-permute-start(s32[128]{0:T(128)S(1)} %copy-done.6), channel_id=1, source_target_pairs={{0,2},{2,4},{4,6},{6,8},{8,10},{10,12},{12,14},{1,3},{3,5},{5,7},{... | collective-permute-start | bytes 1544 | tf_op jit(solution)/shard_map/ppermute | solution.py:31
  22.1 2.6 %collective-permute-start = (bf16[2,128,512]{1,2,0:T(8,128)(2,1)S(1)}, bf16[2,128,512]{1,2,0:T(8,128)(2,1)S(1)}, u32[]{:S(2)}, u32[]{:S(2)}) collective-permute-start(bf16[2,128,512]{1,2,0:T(8,128)(2,1)S(1)} %copy.34), channel_id=1, source_target_pairs={{0,2},{2,4},{4,6},{6,8},{8,10},{10,12},{12,14},{1,3},{3,5},{5,7},{... | collective-permute-start | bytes 786440 | tf_op jit(solution)/shard_map/ppermute | solution.py:31
  25.3 4.3 %collective-permute-start.3 = (s32[128]{0:T(128)S(1)}, s32[128]{0:T(128)S(1)}, u32[]{:S(2)}, u32[]{:S(2)}) collective-permute-start(s32[128]{0:T(128)S(1)} %collective-permute-done.2), channel_id=1, source_target_pairs={{0,2},{2,4},{4,6},{6,8},{8,10},{10,12},{12,14},{1,3},{3,5},{5,7},{... | collective-permute-start | bytes 1544 | tf_op jit(solution)/shard_map/ppermute | solution.py:31
  29.7 2.4 %collective-permute-done = bf16[2,128,512]{1,2,0:T(8,128)(2,1)S(1)} collective-permute-done((bf16[2,128,512]{1,2,0:T(8,128)(2,1)S(1)}, bf16[2,128,512]{1,2,0:T(8,128)(2,1)S(1)}, u32[]{:S(2)}, u32[]{:S(2)}) %collective-permute-start) | collective-permute-done | bytes 262176 | tf_op jit(solution)/shard_map/ppermute | solution.py:31
  32.1 1.9 %collective-permute-start.1 = (bf16[2,128,512]{1,2,0:T(8,128)(2,1)S(1)}, bf16[2,128,512]{1,2,0:T(8,128)(2,1)S(1)}, u32[]{:S(2)}, u32[]{:S(2)}) collective-permute-start(bf16[2,128,512]{1,2,0:T(8,128)(2,1)S(1)} %collective-permute-done), channel_id=1, source_target_pairs={{0,2},{2,4},{4,6},{6,8},{8,10},{10,12},{12,14},{1,3},{3,5},{5,7},{... | collective-permute-start | bytes 786440 | tf_op jit(solution)/shard_map/ppermute | solution.py:31
  34.3 3.1 %collective-permute-start.7 = (bf16[160,2,512]{2,0,1:T(8,128)(2,1)}, bf16[160,2,512]{2,0,1:T(8,128)(2,1)S(1)}, u32[]{:S(2)}, u32[]{:S(2)}) collective-permute-start(bf16[160,2,512]{2,0,1:T(8,128)(2,1)} %collective-permute-done.5), channel_id=1, source_target_pairs={{0,2},{2,4},{4,6},{6,8},{8,10},{10,12},{12,14},{14,0},{1,3},{3,5},... | collective-permute-start | bytes 983048 | tf_op jit(solution)/shard_map/ppermute | solution.py:20
  37.4 10.4 %collective-permute-done.1 = bf16[2,128,512]{1,2,0:T(8,128)(2,1)S(1)} collective-permute-done((bf16[2,128,512]{1,2,0:T(8,128)(2,1)S(1)}, bf16[2,128,512]{1,2,0:T(8,128)(2,1)S(1)}, u32[]{:S(2)}, u32[]{:S(2)}) %collective-permute-start.1) | collective-permute-done | bytes 262176 | tf_op jit(solution)/shard_map/ppermute | solution.py:31
  49.0 3.2 %collective-permute-done.7 = bf16[160,2,512]{2,0,1:T(8,128)(2,1)S(1)} collective-permute-done((bf16[160,2,512]{2,0,1:T(8,128)(2,1)}, bf16[160,2,512]{2,0,1:T(8,128)(2,1)S(1)}, u32[]{:S(2)}, u32[]{:S(2)}) %collective-permute-start.7) | collective-permute-done | bytes 327712 | tf_op jit(solution)/shard_map/ppermute | solution.py:20
  52.2 2.4 %collective-permute-start.9 = (bf16[160,2,512]{2,0,1:T(8,128)(2,1)S(1)}, bf16[160,2,512]{2,0,1:T(8,128)(2,1)}, u32[]{:S(2)}, u32[]{:S(2)}) collective-permute-start(bf16[160,2,512]{2,0,1:T(8,128)(2,1)S(1)} %collective-permute-done.7), channel_id=1, source_target_pairs={{0,2},{2,4},{4,6},{6,8},{8,10},{10,12},{12,14},{14,0},{1,3},{3,5},... | collective-permute-start | bytes 983048 | tf_op jit(solution)/shard_map/ppermute | solution.py:20
  54.6 3.6 %fusion.65 = (f32[4,8,128]{2,1,0:T(8,128)S(1)}, f32[4,8,128,384]{2,3,1,0:T(8,128)}) fusion(f32[4,384,128,8]{2,1,3,0:T(8,128)S(1)} %fusion.20, pred[128,384]{0,1:T(8,128)(4,1)S(1)} %and_and_fusion), kind=kOutput, calls=%fused_computation.102 | output fusion | flops 9437567 | bytes 12648448 | tf_op jit(solution)/shard_map/sub | solution.py:39
  58.2 4.1 %collective-permute-done.6 = bf16[160,2,512]{2,0,1:T(8,128)(2,1)} collective-permute-done((bf16[160,2,512]{2,0,1:T(8,128)(2,1)}, bf16[160,2,512]{2,0,1:T(8,128)(2,1)}, u32[]{:S(2)}, u32[]{:S(2)}) %collective-permute-start.6) | collective-permute-done | bytes 327712 | tf_op jit(solution)/shard_map/ppermute | solution.py:22
  62.3 2.0 %collective-permute-start.10 = (bf16[160,2,512]{2,0,1:T(8,128)(2,1)}, bf16[160,2,512]{2,0,1:T(8,128)(2,1)S(1)}, u32[]{:S(2)}, u32[]{:S(2)}) collective-permute-start(bf16[160,2,512]{2,0,1:T(8,128)(2,1)} %collective-permute-done.9), channel_id=1, source_target_pairs={{0,2},{2,4},{4,6},{6,8},{8,10},{10,12},{12,14},{14,0},{1,3},{3,5},... | collective-permute-start | bytes 983048 | tf_op jit(solution)/shard_map/ppermute | solution.py:20
  64.4 1.6 %multiply_reduce_fusion.1 = f32[256]{0:T(256)S(1)} fusion(f32[256,1280]{1,0:T(8,128)} %all-reduce.2.cloned.1.call-done, bf16[256,1280]{1,0:T(8,128)(2,1)S(1)} %copy-done.2), kind=kLoop, calls=%fused_computation.32 | loop fusion | flops 1310464 | bytes 1967104 | tf_op jit(solution)/shard_map/reduce_sum | solution.py:73
  65.9 1.5 %multiply_convert_fusion.2 = bf16[256,1280]{1,0:T(8,128)(2,1)S(1)} fusion(f32[256,1280]{1,0:T(8,128)} %all-reduce.2.cloned.1.call-done, bf16[256,1280]{1,0:T(8,128)(2,1)S(1)} %copy-done.2, f32[256]{0:T(256)S(1)} %add_rsqrt_fusion), kind=kLoop, calls=%fused_computation.31 | loop fusion | flops 1310720 | bytes 2622464 | tf_op jit(solution)/shard_map/convert_element_type | solution.py:74
  68.2 1.5 %convolution_add_fusion.4 = f32[256,2,512]{2,0,1:T(8,128)S(1)} fusion(f32[256,2,512]{2,0,1:T(8,128)S(1)} %fusion.35, bf16[160,2,512]{2,0,1:T(8,128)(2,1)} %collective-permute-done.4, bf16[256,1280]{1,0:T(8,128)(2,1)S(1)} %multiply_convert_fusion.2, s32[]{:T(128)S(6)} %select_n.75), kind=kOutput, calls=%fused_computation.30 | convolution fusion | flops 84148224 | bytes 2555908 | tf_op jit(solution)/shard_map/ic,cjf->ijf/dot_general | solution.py:79
  69.7 1.3 %convolution_add_fusion.3 = f32[256,2,512]{2,0,1:T(8,128)S(1)} fusion(f32[256,2,512]{2,0,1:T(8,128)S(1)} %convolution_add_fusion.4, bf16[160,2,512]{2,0,1:T(8,128)(2,1)} %collective-permute-done.5, bf16[256,1280]{1,0:T(8,128)(2,1)S(1)} %multiply_convert_fusion.2, s32[]{:T(128)S(6)} %select_n.77), kind=kOutput, calls=%fused_computation.29 | convolution fusion | flops 84148224 | bytes 2555908 | tf_op jit(solution)/shard_map/ic,cjf->ijf/dot_general | solution.py:79
  71.0 1.5 %fusion.15 = f32[256,2,512]{2,0,1:T(8,128)S(1)} fusion(f32[256,2,512]{2,0,1:T(8,128)S(1)} %fusion.30, f32[256,2,512]{2,0,1:T(8,128)S(1)} %convolution_add_fusion.3, bf16[160,2,512]{2,0,1:T(8,128)(2,1)} %collective-permute-done.6, bf16[256,1280]{1,0:T(8,128)(2,1)S(1)} %multiply_convert_fusion.2, s32[]{:T(128)S(6)} %select_n.79), kind=kOutput, calls=%fused_computation.28 | convolution fusion | flops 84410368 | bytes 3604484 | tf_op jit(solution)/shard_map/ic,cjf->ijf/dot_general | solution.py:79
  73.8 5.5 %collective-permute-done.8 = bf16[160,2,512]{2,0,1:T(8,128)(2,1)} collective-permute-done((bf16[160,2,512]{2,0,1:T(8,128)(2,1)}, bf16[160,2,512]{2,0,1:T(8,128)(2,1)}, u32[]{:S(2)}, u32[]{:S(2)}) %collective-permute-start.8) | collective-permute-done | bytes 327712 | tf_op jit(solution)/shard_map/ppermute | solution.py:22
  79.3 1.3 %fusion.14 = f32[256,2,512]{2,0,1:T(8,128)S(1)} fusion(f32[256,2,512]{2,0,1:T(8,128)S(1)} %fusion.27, f32[256,2,512]{2,0,1:T(8,128)S(1)} %fusion.15, bf16[160,2,512]{2,0,1:T(8,128)(2,1)} %collective-permute-done.8, bf16[256,1280]{1,0:T(8,128)(2,1)S(1)} %multiply_convert_fusion.2, s32[]{:T(128)S(6)} %select_n.83), kind=kOutput, calls=%fused_computation.26 | convolution fusion | flops 84410368 | bytes 3604484 | tf_op jit(solution)/shard_map/ic,cjf->ijf/dot_general | solution.py:79
  81.0 2.1 %collective-permute-start.11 = (bf16[256,2,512]{2,0,1:T(8,128)(2,1)S(1)}, bf16[256,2,512]{2,0,1:T(8,128)(2,1)S(1)}, u32[]{:S(2)}, u32[]{:S(2)}) collective-permute-start(bf16[256,2,512]{2,0,1:T(8,128)(2,1)S(1)} %fusion.16), channel_id=1, source_target_pairs={{0,2},{2,4},{4,6},{6,8},{8,10},{10,12},{12,14},{1,3},{3,5},{5,7},{... | collective-permute-start | bytes 1572872 | tf_op jit(solution)/shard_map/ppermute | solution.py:31
  83.1 2.1 %fusion.11 = f32[4,128,8,128]{3,1,2,0:T(8,128)} fusion(bf16[384,4,128,1]{0,2,3,1:T(8,128)(2,1)S(1)} %bitcast.112, f32[4,8,128,384]{2,3,1,0:T(8,128)S(1)} %bitcast.118, f32[4,8,128]{2,1,0:T(8,128)S(1)} %get-tuple-element.14), kind=kOutput, calls=%fused_computation.17 | convolution fusion | flops 405798912 | bytes 8798208 | tf_op jit(solution)/shard_map/ycmq,qyb->mycb/dot_general | solution.py:107
  85.2 2.9 %copy.59 = f32[128,4096]{1,0:T(8,128)} copy(f32[128,4096]{0,1:T(8,128)} %bitcast.108) | data formatting | bytes 4194304 | tf_op jit(solution)/shard_map/reshape | solution.py:113
  88.2 8.6 %collective-permute-done.11 = bf16[256,2,512]{2,0,1:T(8,128)(2,1)S(1)} collective-permute-done((bf16[256,2,512]{2,0,1:T(8,128)(2,1)S(1)}, bf16[256,2,512]{2,0,1:T(8,128)(2,1)S(1)}, u32[]{:S(2)}, u32[]{:S(2)}) %collective-permute-start.11) | collective-permute-done | bytes 524320 | tf_op jit(solution)/shard_map/ppermute | solution.py:31
  97.0 4.5 %fusion.18 = f32[4,512,128,8]{2,1,3,0:T(8,128)} fusion(bf16[128,4,8,128]{3,2,1,0:T(8,128)(2,1)S(1)} %bitcast.105, bf16[512,4,128,1]{2,1,0,3:T(4,128)(2,1)S(1)} %bitcast.106), kind=kOutput, calls=%fused_computation.39 | convolution fusion | flops 536870912 | bytes 9961472 | tf_op jit(solution)/shard_map/tgrd,kgd->grtk/dot_general | solution.py:35
  101.7 8.9 %fusion.67 = (f32[4,8,128]{2,1,0:T(8,128)S(1)}, f32[4,8,128,512]{2,3,1,0:T(8,128)S(1)}) fusion(f32[4,512,128,8]{2,1,3,0:T(8,128)} %fusion.18, pred[128,512]{0,1:T(8,128)(4,1)S(1)} %compare_and_fusion), kind=kOutput, calls=%fused_computation.104 | output fusion | flops 12583423 | bytes 16859136 | tf_op jit(solution)/shard_map/sub | solution.py:39
  110.6 2.3 %fusion.8 = f32[4,128,8,128]{3,1,2,0:T(8,128)} fusion(bf16[512,4,128,1]{0,2,3,1:T(8,128)(2,1)S(1)} %bitcast.111, f32[4,8,128,512]{2,3,1,0:T(8,128)S(1)} %get-tuple-element.19, f32[128]{0:T(128)S(1)} %compare_convert_fusion, f32[4,8,128]{2,1,0:T(8,128)S(1)} %get-tuple-element.18), kind=kOutput, calls=%fused_computation.14 | convolution fusion | flops 543162368 | bytes 11026944 | tf_op jit(solution)/shard_map/ycmq,qyb->mycb/dot_general | solution.py:127
  113.0 3.0 %copy.58 = f32[128,4096]{1,0:T(8,128)} copy(f32[128,4096]{0,1:T(8,128)} %bitcast.107) | data formatting | bytes 4194304 | tf_op jit(solution)/shard_map/reshape | solution.py:133
  116.0 3.5 %add_convert_fusion = bf16[128,4096]{1,0:T(8,128)(2,1)} fusion(f32[128,4096]{1,0:T(8,128)} %copy.59, f32[128,4096]{1,0:T(8,128)} %copy.58, f32[4096]{0:T(1024)S(1)} %broadcast_bitcast_fusion), kind=kLoop, calls=%fused_computation.19 | loop fusion | flops 1572864 | bytes 5259264 | tf_op jit(solution)/shard_map/convert_element_type | solution.py:135
  (64 shorter events, 8.6 us)
Async XLA Ops:
  6.5 9.2 %copy-start = (bf16[640,1280]{1,0:T(8,128)(2,1)S(1)}, bf16[640,1280]{1,0:T(8,128)(2,1)}, u32[]{:S(2)}) copy-start(bf16[640,1280]{1,0:T(8,128)(2,1)} %param.15) | copy-start | bytes 4915204
  6.5 57.8 %all-reduce.2.cloned.1.call-start = ((), (), s32[]{:S(2)}) async-start(), calls=%async_computation | async-start | bytes 2621440 | tf_op jit(solution)/shard_map/psum | solution.py:71
  7.7 29.7 %collective-permute-start.4 = (bf16[160,2,512]{2,0,1:T(8,128)(2,1)S(1)}, bf16[160,2,512]{2,0,1:T(8,128)(2,1)}, u32[]{:S(2)}, u32[]{:S(2)}) collective-permute-start(bf16[160,2,512]{2,0,1:T(8,128)(2,1)S(1)} %copy.44), channel_id=1, source_target_pairs={{0,14},{2,0},{4,2},{6,4},{8,6},{10,8},{12,10},{14,12},{1,15},{3,1}... | collective-permute-start | bytes 983048 | tf_op jit(solution)/shard_map/ppermute | solution.py:22
  9.1 25.2 %collective-permute-start.5 = (bf16[160,2,512]{2,0,1:T(8,128)(2,1)S(1)}, bf16[160,2,512]{2,0,1:T(8,128)(2,1)}, u32[]{:S(2)}, u32[]{:S(2)}) collective-permute-start(bf16[160,2,512]{2,0,1:T(8,128)(2,1)S(1)} %copy.44), channel_id=1, source_target_pairs={{0,2},{2,4},{4,6},{6,8},{8,10},{10,12},{12,14},{14,0},{1,3},{3,5},... | collective-permute-start | bytes 983048 | tf_op jit(solution)/shard_map/ppermute | solution.py:20
  15.6 2.0 %copy-start.6 = (s32[128]{0:T(128)S(1)}, s32[128]{0:T(128)}, u32[]{:S(2)}) copy-start(s32[128]{0:T(128)} %param.11) | copy-start | bytes 1540
  15.6 6.3 %copy-start.5 = (bf16[2,128,512]{2,1,0:T(8,128)(2,1)S(1)}, bf16[2,128,512]{2,1,0:T(8,128)(2,1)}, u32[]{:S(2)}) copy-start(bf16[2,128,512]{2,1,0:T(8,128)(2,1)} %param.10) | copy-start | bytes 786436
  15.6 9.0 %copy-start.7 = (s32[128,2]{0,1:T(2,128)S(1)}, s32[128,2]{0,1:T(2,128)}, u32[]{:S(2)}) copy-start(s32[128,2]{0,1:T(2,128)} %param.12) | copy-start | bytes 3076
  15.7 9.1 %copy-start.8 = (f32[32]{0:T(128)S(1)}, f32[32]{0:T(128)}, u32[]{:S(2)}) copy-start(f32[32]{0:T(128)} %param.17) | copy-start | bytes 388
  15.7 9.4 %copy-start.4 = (bf16[128,4096]{1,0:T(8,128)(2,1)S(1)}, bf16[128,4096]{1,0:T(8,128)(2,1)}, u32[]{:S(2)}) copy-start(bf16[128,4096]{1,0:T(8,128)(2,1)} %param.9) | copy-start | bytes 3145732
  17.6 7.7 %collective-permute-start.2 = (s32[128]{0:T(128)S(1)}, s32[128]{0:T(128)S(1)}, u32[]{:S(2)}, u32[]{:S(2)}) collective-permute-start(s32[128]{0:T(128)S(1)} %copy-done.6), channel_id=1, source_target_pairs={{0,2},{2,4},{4,6},{6,8},{8,10},{10,12},{12,14},{1,3},{3,5},{5,7},{... | collective-permute-start | bytes 1544 | tf_op jit(solution)/shard_map/ppermute | solution.py:31
  22.1 10.0 %collective-permute-start = (bf16[2,128,512]{1,2,0:T(8,128)(2,1)S(1)}, bf16[2,128,512]{1,2,0:T(8,128)(2,1)S(1)}, u32[]{:S(2)}, u32[]{:S(2)}) collective-permute-start(bf16[2,128,512]{1,2,0:T(8,128)(2,1)S(1)} %copy.34), channel_id=1, source_target_pairs={{0,2},{2,4},{4,6},{6,8},{8,10},{10,12},{12,14},{1,3},{3,5},{5,7},{... | collective-permute-start | bytes 786440 | tf_op jit(solution)/shard_map/ppermute | solution.py:31
  25.3 8.7 %collective-permute-start.3 = (s32[128]{0:T(128)S(1)}, s32[128]{0:T(128)S(1)}, u32[]{:S(2)}, u32[]{:S(2)}) collective-permute-start(s32[128]{0:T(128)S(1)} %collective-permute-done.2), channel_id=1, source_target_pairs={{0,2},{2,4},{4,6},{6,8},{8,10},{10,12},{12,14},{1,3},{3,5},{5,7},{... | collective-permute-start | bytes 1544 | tf_op jit(solution)/shard_map/ppermute | solution.py:31
  32.1 15.6 %collective-permute-start.1 = (bf16[2,128,512]{1,2,0:T(8,128)(2,1)S(1)}, bf16[2,128,512]{1,2,0:T(8,128)(2,1)S(1)}, u32[]{:S(2)}, u32[]{:S(2)}) collective-permute-start(bf16[2,128,512]{1,2,0:T(8,128)(2,1)S(1)} %collective-permute-done), channel_id=1, source_target_pairs={{0,2},{2,4},{4,6},{6,8},{8,10},{10,12},{12,14},{1,3},{3,5},{5,7},{... | collective-permute-start | bytes 786440 | tf_op jit(solution)/shard_map/ppermute | solution.py:31
  34.3 17.9 %collective-permute-start.7 = (bf16[160,2,512]{2,0,1:T(8,128)(2,1)}, bf16[160,2,512]{2,0,1:T(8,128)(2,1)S(1)}, u32[]{:S(2)}, u32[]{:S(2)}) collective-permute-start(bf16[160,2,512]{2,0,1:T(8,128)(2,1)} %collective-permute-done.5), channel_id=1, source_target_pairs={{0,2},{2,4},{4,6},{6,8},{8,10},{10,12},{12,14},{14,0},{1,3},{3,5},... | collective-permute-start | bytes 983048 | tf_op jit(solution)/shard_map/ppermute | solution.py:20
  37.4 25.0 %collective-permute-start.6 = (bf16[160,2,512]{2,0,1:T(8,128)(2,1)}, bf16[160,2,512]{2,0,1:T(8,128)(2,1)}, u32[]{:S(2)}, u32[]{:S(2)}) collective-permute-start(bf16[160,2,512]{2,0,1:T(8,128)(2,1)} %collective-permute-done.4), channel_id=1, source_target_pairs={{0,14},{2,0},{4,2},{6,4},{8,6},{10,8},{12,10},{14,12},{1,15},{3,1}... | collective-permute-start | bytes 983048 | tf_op jit(solution)/shard_map/ppermute | solution.py:22
  49.0 15.4 %copy-start.2 = (bf16[256,1280]{1,0:T(8,128)(2,1)S(1)}, bf16[256,1280]{1,0:T(8,128)(2,1)}, u32[]{:S(2)}) copy-start(bf16[256,1280]{1,0:T(8,128)(2,1)} %param.13) | copy-start | bytes 1966084
  52.2 10.1 %collective-permute-start.9 = (bf16[160,2,512]{2,0,1:T(8,128)(2,1)S(1)}, bf16[160,2,512]{2,0,1:T(8,128)(2,1)}, u32[]{:S(2)}, u32[]{:S(2)}) collective-permute-start(bf16[160,2,512]{2,0,1:T(8,128)(2,1)S(1)} %collective-permute-done.7), channel_id=1, source_target_pairs={{0,2},{2,4},{4,6},{6,8},{8,10},{10,12},{12,14},{14,0},{1,3},{3,5},... | collective-permute-start | bytes 983048 | tf_op jit(solution)/shard_map/ppermute | solution.py:20
  58.2 9.3 %copy-start.3 = (bf16[160,2,512]{2,1,0:T(2,128)(2,1)S(1)}, bf16[160,2,512]{2,1,0:T(2,128)(2,1)}, u32[]{:S(2)}) copy-start(bf16[160,2,512]{2,1,0:T(2,128)(2,1)} %param.16) | copy-start | bytes 983044
  62.3 17.0 %collective-permute-start.8 = (bf16[160,2,512]{2,0,1:T(8,128)(2,1)}, bf16[160,2,512]{2,0,1:T(8,128)(2,1)}, u32[]{:S(2)}, u32[]{:S(2)}) collective-permute-start(bf16[160,2,512]{2,0,1:T(8,128)(2,1)} %collective-permute-done.6), channel_id=1, source_target_pairs={{0,14},{2,0},{4,2},{6,4},{8,6},{10,8},{12,10},{14,12},{1,15},{3,1}... | collective-permute-start | bytes 983048 | tf_op jit(solution)/shard_map/ppermute | solution.py:22
  62.3 18.3 %collective-permute-start.10 = (bf16[160,2,512]{2,0,1:T(8,128)(2,1)}, bf16[160,2,512]{2,0,1:T(8,128)(2,1)S(1)}, u32[]{:S(2)}, u32[]{:S(2)}) collective-permute-start(bf16[160,2,512]{2,0,1:T(8,128)(2,1)} %collective-permute-done.9), channel_id=1, source_target_pairs={{0,2},{2,4},{4,6},{6,8},{8,10},{10,12},{12,14},{14,0},{1,3},{3,5},... | collective-permute-start | bytes 983048 | tf_op jit(solution)/shard_map/ppermute | solution.py:20
  68.2 14.9 %slice-start = ((s8[6291456]{0:T(1024)(128)(4,1)}), s8[4194304]{0:T(1024)(128)(4,1)S(1)}, s32[]{:S(2)}) async-start(s8[6291456]{0:T(1024)(128)(4,1)} %bitcast.117), calls=%async_computation.1 | async-start | bytes 8388608
  71.0 12.1 %slice-start.1 = ((s8[6291456]{0:T(1024)(128)(4,1)}), s8[2097152]{0:T(1024)(128)(4,1)S(1)}, s32[]{:S(2)}) async-start(s8[6291456]{0:T(1024)(128)(4,1)} %bitcast.117), calls=%async_computation.2 | async-start | bytes 4194304
  81.0 15.8 %collective-permute-start.11 = (bf16[256,2,512]{2,0,1:T(8,128)(2,1)S(1)}, bf16[256,2,512]{2,0,1:T(8,128)(2,1)S(1)}, u32[]{:S(2)}, u32[]{:S(2)}) collective-permute-start(bf16[256,2,512]{2,0,1:T(8,128)(2,1)S(1)} %fusion.16), channel_id=1, source_target_pairs={{0,2},{2,4},{4,6},{6,8},{8,10},{10,12},{12,14},{1,3},{3,5},{5,7},{... | collective-permute-start | bytes 1572872 | tf_op jit(solution)/shard_map/ppermute | solution.py:31
  113.0 6.5 %copy-start.1 = (bf16[640,1280]{1,0:T(8,128)(2,1)S(1)}, bf16[640,1280]{1,0:T(8,128)(2,1)}, u32[]{:S(2)}) copy-start(bf16[640,1280]{1,0:T(8,128)(2,1)} %param.15) | copy-start | bytes 4915204
Sparse Core Ops, SparseCore 0:
  17.7 24.1 all-reduce.1
